TPU v7x, 32 devices: a whole 2x2x4 slice. The times are simulated.
32 devices in a mesh: row: 8 (over z, core), col: 4 (over y, x).
Axes of the slice: x: 2, y: 2, z: 4, core: 2. Of those that a mesh axis runs over, the one named last changes fastest.
Arguments:
- factor: bfloat16 [16, 1536, 6144], P(None, 'row'), may hold values from -0.078125 to 0.078125
- inverse_blocks: bfloat16 [4, 1536, 1536], P(None, 'row'), as said below
- right_side: float32 [16, 1536, 2048], P(None, 'row', 'col'), may hold values from -6 to 6
- shape_derivative: float32 [4, 1536, 2048], P(None, 'row', 'col')
Outputs:
- solved: float32 [4, 1536, 2048], P(None, 'row', 'col')
- trailing: float32 [12, 1536, 2048], P(None, 'row', 'col')
- sensitivity: float32 [4, 1536], P(None, 'row')
Inputs may be any that keep to these rules, and one draw needn't show every extreme that they name: inverse_blocks[k] is the inverse supplied for the diagonal block of step k.
All inputs are finite; a program needn't handle non-finite values.
Results may differ from a plain program's by a relative error of at most 0.0045.
Values may be sent and summed in bfloat16 or wider, within the bound.
A program may use at most 128 MiB of HBM per device.

v0:
```python
import jax
import jax.numpy as jnp
from jax import lax
from jax.sharding import PartitionSpec as P


def local(factor, inverse_blocks, right_side, shape_derivative):
    step_count = inverse_blocks.shape[0]
    block_size = inverse_blocks.shape[2]
    solved_list = []
    rounded_list = []
    for step in range(step_count):
        residual = right_side[step]
        if step > 0:
            earlier = jnp.concatenate(rounded_list, axis=0)
            panel = factor[step, :, : step * block_size]
            residual = residual - jnp.dot(panel, earlier, preferred_element_type=jnp.float32)
        gathered = lax.all_gather(residual.astype(jnp.bfloat16), "row", axis=0, tiled=True)
        own_rows = jnp.dot(inverse_blocks[step], gathered, preferred_element_type=jnp.float32)
        spread = lax.all_gather(own_rows.astype(jnp.bfloat16), "row", axis=0, tiled=True)
        own_rows, spread = (own_rows, spread)
        solved_list.append(own_rows)
        rounded_list.append(spread)
    all_solved = jnp.concatenate(rounded_list, axis=0)
    update = jnp.einsum(
        "bij,jq->biq", factor[step_count:], all_solved, preferred_element_type=jnp.float32
    )
    trailing = right_side[step_count:] - update
    solved = jnp.stack(solved_list)
    partial_terms = jnp.sum(solved * shape_derivative, axis=2)
    sensitivity = lax.psum(partial_terms, "col")
    return (solved, trailing, sensitivity)


def solution(mesh):
    placed = (
        P(None, "row", None),
        P(None, "row", None),
        P(None, "row", "col"),
        P(None, "row", "col"),
    )
    return jax.shard_map(
        local,
        mesh=mesh,
        in_specs=placed,
        out_specs=(P(None, "row", "col"), P(None, "row", "col"), P(None, "row")),
        check_vma=False,
    )
```

profile of v0, /device:TPU:0, one launch (start us, length us, event | category | flops | bytes accessed | tf_op | source)
XLA Modules:
  0.0 264.2 jit_solution(7392720922657290454)
XLA Ops:
  7.2 1.7 slice.99
  8.9 0.0 all-gather.10.cloned.1.call-start
  9.0 29.0 %all-gather.24.cloned.1.call-done = bf16[1,1536,512]{2,1,0:T(8,128)(2,1)} async-done(((bf16[1,192,512]{2,1,0:T(8,128)(2,1)}), bf16[1,1536,512]{2,1,0:T(8,128)(2,1)}) %all-gather.24.cloned.1.call-update) | async-done | bytes 1572880 | tf_op jit(solution)/shard_map/all_gather | solution.py:18
  38.0 2.8 %fusion.70 = (bf16[192,512]{1,0:T(8,128)(2,1)}, f32[192,512]{1,0:T(8,128)S(1)}) fusion(bf16[1,1536,512]{2,1,0:T(8,128)(2,1)} %all-gather.24.cloned.1.call-done, bf16[4,192,1536]{2,1,0:T(8,128)(2,1)} %param.5), kind=kOutput, calls=%fused_computation.57 | convolution fusion | flops 302088192 | bytes 2752512 | tf_op jit(solution)/shard_map/dot_general | solution.py:19
  40.8 0.0 all-gather.12.cloned.1.call-start
  40.8 24.7 %all-gather.10.cloned.1.call-done = bf16[1536,512]{1,0:T(8,128)(2,1)} async-done(((bf16[192,512]{1,0:T(8,128)(2,1)}), bf16[1536,512]{1,0:T(8,128)(2,1)}) %all-gather.10.cloned.1.call-update) | async-done | bytes 1572880 | tf_op jit(solution)/shard_map/all_gather | solution.py:20
  65.5 2.8 %fusion.48 = bf16[192,512]{1,0:T(8,128)(2,1)} fusion(bf16[1536,512]{1,0:T(8,128)(2,1)} %all-gather.10.cloned.1.call-done, bf16[16,192,6144]{2,1,0:T(8,128)(2,1)} %param.4, f32[16,192,512]{2,1,0:T(8,128)} %param.6), kind=kOutput, calls=%fused_computation.35 | convolution fusion | flops 302186496 | bytes 2752512 | tf_op jit(solution)/shard_map/dot_general | solution.py:17
  68.3 0.0 all-gather.14.cloned.1.call-start
  68.4 24.7 %all-gather.12.cloned.1.call-done = bf16[1536,512]{1,0:T(8,128)(2,1)} async-done(((bf16[192,512]{1,0:T(8,128)(2,1)}), bf16[1536,512]{1,0:T(8,128)(2,1)}) %all-gather.12.cloned.1.call-update) | async-done | bytes 1572880 | tf_op jit(solution)/shard_map/all_gather | solution.py:18
  93.1 2.6 bitcast_convert_fusion.2
  95.7 0.0 all-gather.16.cloned.1.call-start
  95.7 24.7 %all-gather.14.cloned.1.call-done = bf16[1536,512]{1,0:T(8,128)(2,1)} async-done(((bf16[192,512]{1,0:T(8,128)(2,1)}), bf16[1536,512]{1,0:T(8,128)(2,1)}) %all-gather.14.cloned.1.call-update) | async-done | bytes 1572880 | tf_op jit(solution)/shard_map/all_gather | solution.py:20
  120.4 3.8 %fusion.49 = bf16[192,512]{1,0:T(8,128)(2,1)} fusion(bf16[1536,512]{1,0:T(8,128)(2,1)} %all-gather.14.cloned.1.call-done, bf16[1536,512]{1,0:T(8,128)(2,1)} %all-gather.10.cloned.1.call-done, bf16[16,192,6144]{2,1,0:T(8,128)(2,1)} %param.4, f32[16,192,512]{2,1,0:T(8,128)} %param.6), kind=kOutput, calls=%fused_computation.36 | convolution fusion | flops 610467840 | bytes 4915200 | tf_op jit(solution)/shard_map/dot_general | solution.py:17
  124.2 24.7 %all-gather.16.cloned.1.call-done = bf16[1536,512]{1,0:T(8,128)(2,1)} async-done(((bf16[192,512]{1,0:T(8,128)(2,1)}), bf16[1536,512]{1,0:T(8,128)(2,1)}) %all-gather.16.cloned.1.call-update) | async-done | bytes 1572880 | tf_op jit(solution)/shard_map/all_gather | solution.py:18
  148.9 2.6 bitcast_convert_fusion.1
  151.5 0.0 all-gather.20.cloned.1.call-start
  151.6 24.7 %all-gather.18.cloned.1.call-done = bf16[1536,512]{1,0:T(8,128)(2,1)} async-done(((bf16[192,512]{1,0:T(8,128)(2,1)}), bf16[1536,512]{1,0:T(8,128)(2,1)}) %all-gather.18.cloned.1.call-update) | async-done | bytes 1572880 | tf_op jit(solution)/shard_map/all_gather | solution.py:20
  176.3 4.7 %fusion.43 = bf16[192,512]{1,0:T(8,128)(2,1)} fusion(bf16[1536,512]{1,0:T(8,128)(2,1)} %all-gather.18.cloned.1.call-done, bf16[1536,512]{1,0:T(8,128)(2,1)} %all-gather.14.cloned.1.call-done, bf16[1536,512]{1,0:T(8,128)(2,1)} %all-gather.10.cloned.1.call-done, bf16[16,192,6144]{2,1,0:T(8,128)(2,1)} %param.4, f32[16,192,512]{2,1,0:T(8,128)} %param.6), kind=kOutput, calls=%fused_computation.34 | convolution fusion | flops 920322048 | bytes 7077888 | tf_op jit(solution)/shard_map/dot_general | solution.py:17
  181.0 24.7 %all-gather.20.cloned.1.call-done = bf16[1536,512]{1,0:T(8,128)(2,1)} async-done(((bf16[192,512]{1,0:T(8,128)(2,1)}), bf16[1536,512]{1,0:T(8,128)(2,1)}) %all-gather.20.cloned.1.call-update) | async-done | bytes 1572880 | tf_op jit(solution)/shard_map/all_gather | solution.py:18
  205.7 2.7 %bitcast_convert_fusion = (bf16[192,512]{1,0:T(8,128)(2,1)}, f32[512,192]{0,1:T(8,128)}) fusion(bf16[1536,512]{1,0:T(8,128)(2,1)} %all-gather.20.cloned.1.call-done, bf16[4,192,1536]{2,1,0:T(8,128)(2,1)S(1)} %copy-done), kind=kOutput, calls=%fused_computation.51 | convolution fusion | flops 302088192 | bytes 2752512 | tf_op jit(solution)/shard_map/dot_general | solution.py:19
  208.4 2.9 %multiply_reduce_fusion = (f32[4,192]{1,0:T(4,128)S(1)}, f32[4,192,512]{2,1,0:T(8,128)}) fusion(f32[4,192,512]{2,1,0:T(8,128)} %param.7, f32[1,192,512]{2,1,0:T(8,128)} %bitcast.93, f32[1,192,512]{2,1,0:T(8,128)S(1)} %bitcast.92, f32[1,192,512]{2,1,0:T(8,128)S(1)} %bitcast.91, f32[1,192,512]{2,1,0:T(8,128)S(1)} %bitcast.90), kind=kLoop, calls=%fused_computation.25 | loop fusion | flops 1965312 | bytes 4721664 | tf_op jit(solution)/shard_map/reduce_sum | solution.py:30
  211.3 10.4 %psum.7 = f32[4,192]{1,0:T(4,128)} all-reduce(f32[4,192]{1,0:T(4,128)S(1)} %get-tuple-element.3), channel_id=1, replica_groups=mesh['row'=8,'col'=4] {'col'}, use_global_device_ids=true, to_apply=%region_1.0 | all-reduce | flops 768 | bytes 6144 | tf_op jit(solution)/shard_map/psum | solution.py:31
  221.7 11.4 %all-gather.22.cloned.1.call-done = bf16[1536,512]{1,0:T(8,128)(2,1)} async-done(((bf16[192,512]{1,0:T(8,128)(2,1)}), bf16[1536,512]{1,0:T(8,128)(2,1)}) %all-gather.22.cloned.1.call-update) | async-done | bytes 1572880 | tf_op jit(solution)/shard_map/all_gather | solution.py:20
  233.2 24.2 %bitcast_subtract_fusion = f32[12,192,512]{2,1,0:T(8,128)} fusion(f32[16,192,512]{2,1,0:T(8,128)} %param.6, bf16[16,192,6144]{2,1,0:T(8,128)(2,1)} %param.4, bf16[1536,512]{1,0:T(8,128)(2,1)} %all-gather.22.cloned.1.call-done, bf16[1536,512]{1,0:T(8,128)(2,1)} %all-gather.18.cloned.1.call-done, bf16[1536,512]{1,0:T(8,128)(2,1)} %all-gather.14.cloned.1.call-done, ...), kind=kOutput, calls=%fused_computation.15 | convolution fusion | flops 14521860096 | bytes 44040192 | tf_op jit(solution)/shard_map/bij,jq->biq/dot_general | solution.py:25
  (15 shorter events, 0.3 us)
Async XLA Ops:
  7.2 30.8 %all-gather.24.cloned.1.call-start = ((), (), s32[]{:S(2)}) async-start(), calls=%async_computation.7 | async-start | bytes 1769472 | tf_op jit(solution)/shard_map/all_gather | solution.py:18
  8.9 84.2 %copy-start = (bf16[4,192,1536]{2,1,0:T(8,128)(2,1)S(1)}, bf16[4,192,1536]{2,1,0:T(8,128)(2,1)}, u32[]{:S(2)}) copy-start(bf16[4,192,1536]{2,1,0:T(8,128)(2,1)} %param.5) | copy-start | bytes 7077892
  8.9 56.6 %all-gather.10.cloned.1.call-start = ((), (), s32[]{:S(2)}) async-start(), calls=%async_computation | async-start | bytes 1769472 | tf_op jit(solution)/shard_map/all_gather | solution.py:20
  40.8 52.3 %all-gather.12.cloned.1.call-start = ((), (), s32[]{:S(2)}) async-start(), calls=%async_computation.1 | async-start | bytes 1769472 | tf_op jit(solution)/shard_map/all_gather | solution.py:18
  68.3 52.1 %all-gather.14.cloned.1.call-start = ((), (), s32[]{:S(2)}) async-start(), calls=%async_computation.2 | async-start | bytes 1769472 | tf_op jit(solution)/shard_map/all_gather | solution.py:20
  95.7 53.3 %all-gather.16.cloned.1.call-start = ((), (), s32[]{:S(2)}) async-start(), calls=%async_computation.3 | async-start | bytes 1769472 | tf_op jit(solution)/shard_map/all_gather | solution.py:18
  124.2 52.1 %all-gather.18.cloned.1.call-start = ((), (), s32[]{:S(2)}) async-start(), calls=%async_computation.4 | async-start | bytes 1769472 | tf_op jit(solution)/shard_map/all_gather | solution.py:20
  151.5 54.2 %all-gather.20.cloned.1.call-start = ((), (), s32[]{:S(2)}) async-start(), calls=%async_computation.5 | async-start | bytes 1769472 | tf_op jit(solution)/shard_map/all_gather | solution.py:18
  181.0 52.2 %all-gather.22.cloned.1.call-start = ((), (), s32[]{:S(2)}) async-start(), calls=%async_computation.6 | async-start | bytes 1769472 | tf_op jit(solution)/shard_map/all_gather | solution.py:20
  208.4 24.7 %copy-start.1 = (bf16[1536,512]{1,0:T(8,128)(2,1)S(1)}, bf16[1536,512]{1,0:T(8,128)(2,1)}, u32[]{:S(2)}) copy-start(bf16[1536,512]{1,0:T(8,128)(2,1)} %all-gather.10.cloned.1.call-done) | copy-start | bytes 4718596
Sparse Core Ops, SparseCore 0:
  10.2 27.7 all-gather.23
  40.9 24.5 all-gather.9
  68.5 24.5 all-gather.11
  95.8 24.5 all-gather.13
  124.3 24.5 all-gather.15
  151.6 24.5 all-gather.17
  181.1 24.5 all-gather.19
  208.6 24.5 all-gather.21
where the time goes:
time: 265 us; the launch traced here: 264 us
  waiting for transfers between devices  189 us (71%)
  matrix products  46 us (17%)
  between operations  14.2 us (5%)
  blocking collectives  10.4 us (4%)
  other arithmetic  2.89 us (1%)
    all_gather x4, waiting for transfers between devices, local(): lax.all_gather(residual.astype(jnp.bfloat16), 'row', axis=0, tiled=True)  103 us
    all_gather x4, waiting for transfers between devices, local(): lax.all_gather(own_rows.astype(jnp.bfloat16), 'row', axis=0, tiled=True)  85.5 us
    dot_general x1, matrix products, local(): jnp.einsum('bij,jq->biq', factor[step_count:], all_solved, preferred_elem...  24.2 us
    dot_general x3, matrix products, local(): jnp.dot(panel, earlier, preferred_element_type=jnp.float32)  11.2 us
    dot_general x4, matrix products, local(): jnp.dot(inverse_blocks[step], gathered, preferred_element_type=jnp.float32)  10.6 us
    psum x1, blocking collectives, local(): sensitivity = lax.psum(partial_terms, 'col')  10.4 us
  transfers between devices with their start and end apart: 8, of which 8 were waited for; matrix products, arithmetic and copies ran while one was open for 1% of the time, Pallas kernels for 0%

commit v1 on v0

v1 whole, which is shorter than its diff:
```python
import functools

import jax
import jax.numpy as jnp
from jax import lax
from jax.experimental import pallas as pl
from jax.experimental.pallas import tpu as pltpu
from jax.sharding import PartitionSpec as P

HALVES = 2
FULL_STEPS = 1
F32 = jnp.float32
BF16 = jnp.bfloat16
SIB, UP, DOWN = 0, 1, 2


def mm(a, b):
    return jnp.dot(a, b, preferred_element_type=F32)


def kernel(
    chips, peers,
    factor, inverse, right, deriv,
    solved_out, trailing_out, sens_out,
    panel, inv, end_inv, tail, racc, tacc, sd, sol, rbuf, xbuf, sacc, sens,
    load_sem, store_sem, end_sem, r_recv, x_recv, send_sem, peer_send, peer_recv,
):
    steps, rows, size = inv.shape
    halves, cols = racc.shape[0], racc.shape[3]
    blocks = tacc.shape[1]
    ranks = 2 * chips
    me = lax.axis_index("row")
    z = me // 2
    c = lax.rem(me, 2)
    other = 1 - c
    mine = lax.axis_index("col")
    last = chips - 1

    def low(k):
        return 0 if k < FULL_STEPS else 1

    loads = {}

    def load(name, src, dst):
        copy = pltpu.make_async_copy(src, dst, load_sem.at[len(loads)])
        copy.start()
        loads[name] = [copy, False]

    def ready(name):
        entry = loads[name]
        if not entry[1]:
            entry[0].wait()
            entry[1] = True

    def columns(h):
        return pl.ds(h * cols, cols)

    for h in range(halves):
        load(("r", h), right.at[pl.ds(0, steps), :, columns(h)], racc.at[h])

    def at_row(chip, core):
        return {"row": 2 * chip + core}

    barrier = pltpu.get_barrier_semaphore()

    def greet(chip, core):
        pl.semaphore_signal(
            barrier, inc=1, device_id=at_row(chip, core), device_id_type=pl.DeviceIdType.MESH
        )

    greet(z, other)
    for t in range(1, peers):
        pl.semaphore_signal(
            barrier, inc=1, device_id={"col": lax.rem(mine + t, peers)},
            device_id_type=pl.DeviceIdType.MESH,
        )
    pl.when(z > 0)(lambda: greet(z - 1, c))
    pl.when(z < last)(lambda: greet(z + 1, c))

    load(("inv", 0), inverse.at[0], inv.at[0])
    pairs = [(k, j) for j in range(steps) for k in range(j + 1, steps)]
    place = {pair: n for n, pair in enumerate(pairs)}
    for j in range(steps):
        for k in range(j + 1, steps):
            load(("panel", k, j), factor.at[k, :, pl.ds(j * size, size)], panel.at[place[k, j]])
        if j == 0:
            for h in range(halves):
                load(("d", h), deriv.at[:, :, columns(h)], sd.at[h])
            for h in range(halves):
                load(("t", h), right.at[pl.ds(steps, blocks), :, columns(h)], tacc.at[h])
        load(("tail", j), factor.at[pl.ds(steps, blocks), :, pl.ds(j * size, size)], tail.at[j])
        if j + 1 < steps:
            load(("inv", j + 1), inverse.at[j + 1], inv.at[j + 1])

    neighbours = jnp.where(z > 0, 1, 0) + jnp.where(z < last, 1, 0)
    pl.semaphore_wait(barrier, peers + neighbours)

    def shard(kind, k, h, index, direction):
        buffer, recv = (rbuf, r_recv) if kind == 0 else (xbuf, x_recv)
        chip, core = [(z, other), (z + 1, c), (z - 1, c)][direction]
        return pltpu.make_async_remote_copy(
            src_ref=buffer.at[k, h, index],
            dst_ref=buffer.at[k, h, index],
            send_sem=send_sem.at[kind, k, h, index, direction],
            recv_sem=recv.at[k, h, index],
            device_id=at_row(chip, core),
            device_id_type=pl.DeviceIdType.MESH,
        )

    def send(kind, k, h, chip, direction):
        shard(kind, k, h, 2 * chip + c, direction).start()

    def received(kind, k, h, chip, core):
        shard(kind, k, h, 2 * chip + core, SIB).wait_recv()

    def end_copy(k, target):
        n = k - FULL_STEPS
        return pltpu.make_async_remote_copy(
            src_ref=inverse.at[k], dst_ref=end_inv.at[n],
            send_sem=end_sem.at[0, n], recv_sem=end_sem.at[1, n],
            device_id=at_row(target, c), device_id_type=pl.DeviceIdType.MESH,
        )

    def send_own_r(k, h):
        lo = low(k)
        hi = last - lo
        pl.when(z + 1 <= hi)(lambda: send(0, k, h, z, UP))
        pl.when(z - 1 >= lo)(lambda: send(0, k, h, z, DOWN))
        pl.when((z >= lo) & (z <= hi))(lambda: send(0, k, h, z, SIB))

    def take_r(k, h):
        lo = low(k)
        hi = last - lo

        def gather():
            for t in range(1, chips):
                for d in (1, -1):
                    s = z - d * t

                    def arrive(s=s, d=d):
                        received(0, k, h, s, c)
                        onward = (z + 1 <= hi) if d == 1 else (z - 1 >= lo)
                        pl.when(onward)(lambda: send(0, k, h, s, UP if d == 1 else DOWN))
                        send(0, k, h, s, SIB)

                    pl.when((s >= 0) & (s <= last))(arrive)
            for s in range(chips):
                received(0, k, h, s, other)

        if lo == 0:
            gather()
        else:
            pl.when((z >= lo) & (z <= hi))(gather)

    def send_own_x(k, h, s):
        pl.when(z < last)(lambda: send(1, k, h, s, UP))
        pl.when(z > 0)(lambda: send(1, k, h, s, DOWN))
        send(1, k, h, s, SIB)

    def solve(k, h):
        lo = low(k)
        hi = last - lo
        ready(("inv", k))

        def own():
            gathered = rbuf[k, h].reshape(ranks * rows, cols)
            value = mm(inv[k], gathered)
            sol[h, k] = value
            xbuf[k, h, me] = value.astype(BF16)
            send_own_x(k, h, z)

        def for_end():
            n = k - FULL_STEPS
            if h == 0:
                end_copy(k, z).wait_recv()
            end = jnp.where(z == lo, 0, last)
            gathered = rbuf[k, h].reshape(ranks * rows, cols)
            xbuf[k, h, 2 * end + c] = mm(end_inv[n], gathered).astype(BF16)
            send_own_x(k, h, end)

        if lo == 0:
            own()
        else:
            pl.when((z >= lo) & (z <= hi))(own)
            pl.when((z == lo) | (z == hi))(for_end)

    def take_x(k, h):
        lo = low(k)
        hi = last - lo
        for t in range(1, chips):
            for d in (1, -1):
                home = z - d * t

                def arrive(s, d=d):
                    received(1, k, h, s, c)
                    onward = (z + 1 <= last) if d == 1 else (z - 1 >= 0)
                    pl.when(onward)(lambda: send(1, k, h, s, UP if d == 1 else DOWN))
                    send(1, k, h, s, SIB)

                pl.when((home >= lo) & (home <= hi))(lambda home=home, arrive=arrive: arrive(home))
                if lo == 1:
                    pl.when(home == lo)(lambda arrive=arrive: arrive(0))
                    pl.when(home == hi)(lambda arrive=arrive: arrive(last))
        for s in range(chips):
            received(1, k, h, s, other)
        if lo == 1:

            def widen():
                sol[h, k] = xbuf[k, h, me].astype(F32)

            pl.when((z < lo) | (z > hi))(widen)

    stores = []

    def store(src, dst):
        copy = pltpu.make_async_copy(src, dst, store_sem.at[len(stores)])
        copy.start()
        stores.append(copy)

    def spread(k, h):
        return xbuf[k, h].reshape(ranks * rows, cols)

    def next_r(k, h):
        ready(("panel", k + 1, k))
        value = racc[h, k + 1] - mm(panel[place[k + 1, k]], spread(k, h))
        rbuf[k + 1, h, me] = value.astype(BF16)
        send_own_r(k + 1, h)

    group = max(g for g in (4, 3, 2, 1) if blocks % g == 0)

    def finish(k, h):
        for m in range(k + 2, steps):
            ready(("panel", m, k))
            racc[h, m] -= mm(panel[place[m, k]], spread(k, h))
        ready(("t", h))
        ready(("tail", k))

        def update(i, carry):
            span = pl.ds(i * group, group)
            part = mm(tail[k, span].reshape(group * rows, size), spread(k, h))
            tacc[h, span] -= part.reshape(group, rows, cols)
            return carry

        lax.fori_loop(0, blocks // group, update, 0)
        if k == steps - 1:
            store(tacc.at[h], trailing_out.at[:, :, columns(h)])

    def sensitivity(k, h):
        ready(("d", h))
        store(sol.at[h, k], solved_out.at[k, :, columns(h)])
        part = jnp.sum(sol[h, k] * sd[h, k], axis=1, keepdims=True)
        lane = lax.broadcasted_iota(jnp.int32, (rows, 128), 1)
        sacc[...] += jnp.where(lane == k, part, 0.0)

    sacc[...] = jnp.zeros_like(sacc)
    for h in range(halves):
        ready(("r", h))
        rbuf[0, h, me] = racc[h, 0].astype(BF16)
        send_own_r(0, h)
    for k in range(FULL_STEPS, steps):
        pl.when(z == 0)(lambda k=k: end_copy(k, 1).start())
        pl.when(z == last)(lambda k=k: end_copy(k, last - 1).start())

    pending = None
    for k in range(steps):
        for h in range(halves):
            take_r(k, h)
            solve(k, h)
            if pending is not None:
                finish(*pending)
                sensitivity(*pending)
            take_x(k, h)
            if k + 1 < steps:
                next_r(k, h)
            pending = (k, h)
    sensitivity(*pending)
    sens[mine] = sacc[...]
    shares = []
    for t in range(1, peers):
        copy = pltpu.make_async_remote_copy(
            src_ref=sens.at[mine], dst_ref=sens.at[mine],
            send_sem=peer_send.at[t], recv_sem=peer_recv.at[t],
            device_id={"col": lax.rem(mine + t, peers)},
            device_id_type=pl.DeviceIdType.MESH,
        )
        copy.start()
        shares.append(copy)
    finish(*pending)
    for copy in shares:
        copy.wait()
    total = sens[0]
    for j in range(1, peers):
        total = total + sens[j]
    sens_out[...] = total

    def drain(n, carry):
        p = n // chips
        s = lax.rem(n, chips)
        k = p // halves
        h = lax.rem(p, halves)
        lo = jnp.where(k < FULL_STEPS, 0, 1)
        hi = last - lo
        home = jnp.clip(s, lo, hi)
        index = 2 * s + c

        def left(kind, direction):
            return lambda: shard(kind, k, h, index, direction).wait_send()

        pl.when((z >= lo) & (z <= hi))(left(0, SIB))
        pl.when((s <= z) & (z + 1 <= hi))(left(0, UP))
        pl.when((s >= z) & (z - 1 >= lo))(left(0, DOWN))
        left(1, SIB)()
        pl.when((home <= z) & (z + 1 <= last))(left(1, UP))
        pl.when((home >= z) & (z - 1 >= 0))(left(1, DOWN))
        return carry

    lax.fori_loop(0, steps * halves * chips, drain, 0)
    for k in range(FULL_STEPS, steps):
        pl.when((z == 0) | (z == last))(lambda k=k: end_copy(k, 1).wait_send())
    for copy in stores:
        copy.wait()


def local(chips, peers, factor, inverse_blocks, right_side, shape_derivative):
    steps, rows, size = inverse_blocks.shape
    blocks = factor.shape[0] - steps
    width = right_side.shape[2]
    cols = width // HALVES
    ranks = 2 * chips
    pairs = steps * (steps - 1) // 2
    ends = steps - FULL_STEPS
    multiplied = (pairs + steps * blocks) * rows * size * width + steps * rows * size * width
    anywhere = pl.BlockSpec(memory_space=pl.ANY)
    dma = pltpu.SemaphoreType.DMA
    solved, trailing, sens = pl.pallas_call(
        functools.partial(kernel, chips, peers),
        out_shape=(
            jax.ShapeDtypeStruct((steps, rows, width), F32),
            jax.ShapeDtypeStruct((blocks, rows, width), F32),
            jax.ShapeDtypeStruct((rows, 128), F32),
        ),
        in_specs=[anywhere] * 4,
        out_specs=(anywhere, anywhere, pl.BlockSpec(memory_space=pltpu.VMEM)),
        scratch_shapes=[
            pltpu.VMEM((pairs, rows, size), BF16),
            pltpu.VMEM((steps, rows, size), BF16),
            pltpu.VMEM((ends, rows, size), BF16),
            pltpu.VMEM((steps, blocks, rows, size), BF16),
            pltpu.VMEM((HALVES, steps, rows, cols), F32),
            pltpu.VMEM((HALVES, blocks, rows, cols), F32),
            pltpu.VMEM((HALVES, steps, rows, cols), F32),
            pltpu.VMEM((HALVES, steps, rows, cols), F32),
            pltpu.VMEM((steps, HALVES, ranks, rows, cols), BF16),
            pltpu.VMEM((steps, HALVES, ranks, rows, cols), BF16),
            pltpu.VMEM((rows, 128), F32),
            pltpu.VMEM((peers, rows, 128), F32),
            dma((pairs + 2 * steps + 3 * HALVES,)),
            dma((steps * HALVES + HALVES,)),
            dma((2, ends)),
            dma((steps, HALVES, ranks)),
            dma((steps, HALVES, ranks)),
            dma((2, steps, HALVES, ranks, 3)),
            dma((peers,)),
            dma((peers,)),
        ],
        compiler_params=pltpu.CompilerParams(
            collective_id=0, has_side_effects=True, vmem_limit_bytes=63 * 1024 * 1024
        ),
        cost_estimate=pl.CostEstimate(
            flops=2 * multiplied,
            bytes_accessed=2 * factor.size + 2 * inverse_blocks.size + 8 * right_side.size,
            transcendentals=0,
        ),
        name="substitution",
    )(factor, inverse_blocks, right_side, shape_derivative)
    return solved, trailing, sens[:, :steps].T


def solution(mesh):
    chips = mesh.shape["row"] // 2
    peers = mesh.shape["col"]
    return jax.shard_map(
        functools.partial(local, chips, peers),
        mesh=mesh,
        in_specs=(
            P(None, "row", None),
            P(None, "row", None),
            P(None, "row", "col"),
            P(None, "row", "col"),
        ),
        out_specs=(P(None, "row", "col"), P(None, "row", "col"), P(None, "row")),
        check_vma=False,
    )
```

time: 265 us -> 192 us (0.72)
  waiting for transfers between devices: 189 us -> 0 us
  Pallas kernels: 0 us -> 182 us
  matrix products: 46 us -> 0 us
  between operations: 14.2 us -> 0.64 us
  blocking collectives: 10.4 us -> 0 us
  local copies, waits for them, and re-layouts: 1.71 us -> 9.27 us
  other arithmetic: 2.89 us -> 0 us
    all_gather x8 -> x0, waiting for transfers between devices: 189 us -> none  [the longest x4 103 us: local(): lax.all_gather(residual.astype(jnp.bfloat16), 'row', axis=0, tiled=True)]
    pallas_call x0 -> x1, Pallas kernels: none -> 182 us  [local(): pl.pallas_call(functools.partial(kernel, chips, peers), out_shape=(jax.Sh...]
    dot_general x8 -> x0, matrix products: 46 us -> none  [the longest x1 24.2 us: local(): jnp.einsum('bij,jq->biq', factor[step_count:], all_solved, preferred_elem...]
    psum x1 -> x0, blocking collectives: 10.4 us -> none  [local(): sensitivity = lax.psum(partial_terms, 'col')]
    unnamed x4 -> x3, local copies, waits for them, and re-layouts: 0.01 us -> 8.37 us
    reduce_sum x1 -> x0, other arithmetic: 2.89 us -> none  [local(): partial_terms = jnp.sum(solved * shape_derivative, axis=2)]
  transfers between devices with their start and end apart: 8 -> 0, of which waited for: 8 -> 0; matrix products, arithmetic and copies ran while one was open for 1% -> 0% of each run, Pallas kernels for 0% -> 0%
where the time goes in v1:
time: 192 us
  Pallas kernels  182 us (95%)
  local copies, waits for them, and re-layouts  9.27 us (5%)
    pallas_call x1, Pallas kernels, local(): pl.pallas_call(functools.partial(kernel, chips, peers), out_shape=(jax.Sh...  182 us
    unnamed x3, local copies, waits for them, and re-layouts  8.37 us

profile of v1, /device:TPU:0, one launch (start us, length us, event | category | flops | bytes accessed | tf_op | source)
XLA Modules:
  0.0 192.2 jit_solution(8849649677508876412)
XLA Ops:
  0.6 182.3 %substitution.1 = (f32[4,192,512]{2,1,0:T(8,128)}, f32[12,192,512]{2,1,0:T(8,128)}, f32[192,128]{1,0:T(8,128)}) custom-call(bf16[16,192,6144]{2,1,0:T(8,128)(2,1)} %factor.1, bf16[4,192,1536]{2,1,0:T(8,128)(2,1)} %inverse.1, f32[16,192,512]{2,1,0:T(8,128)} %right.1, f32[4,192,512]{2,1,0:T(8,128)} %deriv.1), custom_call_target="tpu_custom_call" | custom-call | flops 17515413504 | bytes 52690944 | tf_op jit(solution)/shard_map/substitution/pallas_call | solution.py:335
  182.9 0.9 slice_bitcast_fusion
  183.8 0.7 copy.7
  184.5 2.7 %copy.10 = f32[4,192,512]{2,1,0:T(8,128)} copy(f32[4,192,512]{2,1,0:T(8,128)} %get-tuple-element.15) | data formatting | bytes 3145728
  187.2 5.0 %copy.11 = f32[12,192,512]{2,1,0:T(8,128)} copy(f32[12,192,512]{2,1,0:T(8,128)} %get-tuple-element.16) | data formatting | bytes 9437184

commit v2 on v1

--- a/solution.py
+++ b/solution.py
@@ -11,7 +11,7 @@
 FULL_STEPS = 1
 F32 = jnp.float32
 BF16 = jnp.bfloat16
-SIB, UP, DOWN = 0, 1, 2
+SIB, UP, DOWN, FAR = 0, 1, 2, 3
 
 
 def mm(a, b):
@@ -23,7 +23,7 @@
     factor, inverse, right, deriv,
     solved_out, trailing_out, sens_out,
     panel, inv, end_inv, tail, racc, tacc, sd, sol, rbuf, xbuf, sacc, sens,
-    load_sem, store_sem, end_sem, r_recv, x_recv, send_sem, peer_send, peer_recv,
+    load_sem, store_sem, end_sem, r_recv, x_recv, send_sem, share_sem, peer_send, peer_recv,
 ):
     steps, rows, size = inv.shape
     halves, cols = racc.shape[0], racc.shape[3]
@@ -76,6 +76,8 @@
         )
     pl.when(z > 0)(lambda: greet(z - 1, c))
     pl.when(z < last)(lambda: greet(z + 1, c))
+    pl.when((z == 0) | (z == last - 2))(lambda: greet(z + 2, c))
+    pl.when((z == last) | (z == 2))(lambda: greet(z - 2, c))
 
     load(("inv", 0), inverse.at[0], inv.at[0])
     pairs = [(k, j) for j in range(steps) for k in range(j + 1, steps)]
@@ -93,11 +95,14 @@
             load(("inv", j + 1), inverse.at[j + 1], inv.at[j + 1])
 
     neighbours = jnp.where(z > 0, 1, 0) + jnp.where(z < last, 1, 0)
+    neighbours += jnp.where((z == 0) | (z == last - 2), 1, 0)
+    neighbours += jnp.where((z == last) | (z == 2), 1, 0)
     pl.semaphore_wait(barrier, peers + neighbours)
 
     def shard(kind, k, h, index, direction):
         buffer, recv = (rbuf, r_recv) if kind == 0 else (xbuf, x_recv)
-        chip, core = [(z, other), (z + 1, c), (z - 1, c)][direction]
+        far = jnp.where(z == 0, 2, last - 2)
+        chip, core = [(z, other), (z + 1, c), (z - 1, c), (far, c)][direction]
         return pltpu.make_async_remote_copy(
             src_ref=buffer.at[k, h, index],
             dst_ref=buffer.at[k, h, index],
@@ -113,10 +118,34 @@
     def received(kind, k, h, chip, core):
         shard(kind, k, h, 2 * chip + core, SIB).wait_recv()
 
+    sharers = max(
+        g for g in range(1, peers + 1) if peers % g == 0 and rows % g == 0 and rows // g % 16 == 0
+    )
+    part_rows = rows // sharers
+    turn = lax.rem(mine, sharers)
+    piece = pl.ds(pl.multiple_of(turn * part_rows, part_rows), part_rows)
+
+    def share(k, t):
+        n = k - FULL_STEPS
+        return pltpu.make_async_remote_copy(
+            src_ref=end_inv.at[n, piece], dst_ref=end_inv.at[n, piece],
+            send_sem=share_sem.at[0, n, t], recv_sem=share_sem.at[1, n, t],
+            device_id={"col": mine - turn + lax.rem(turn + t, sharers)},
+            device_id_type=pl.DeviceIdType.MESH,
+        )
+
+    def share_end(k):
+        def go():
+            end_copy(k, z).wait_recv()
+            for t in range(1, sharers):
+                share(k, t).start()
+
+        pl.when((z == 1) | (z == last - 1))(go)
+
     def end_copy(k, target):
         n = k - FULL_STEPS
         return pltpu.make_async_remote_copy(
-            src_ref=inverse.at[k], dst_ref=end_inv.at[n],
+            src_ref=inverse.at[k, piece], dst_ref=end_inv.at[n, piece],
             send_sem=end_sem.at[0, n], recv_sem=end_sem.at[1, n],
             device_id=at_row(target, c), device_id_type=pl.DeviceIdType.MESH,
         )
@@ -126,7 +155,11 @@
         hi = last - lo
         pl.when(z + 1 <= hi)(lambda: send(0, k, h, z, UP))
         pl.when(z - 1 >= lo)(lambda: send(0, k, h, z, DOWN))
-        pl.when((z >= lo) & (z <= hi))(lambda: send(0, k, h, z, SIB))
+        if lo == 0:
+            send(0, k, h, z, SIB)
+        else:
+            pl.when((z >= lo) & (z <= hi))(lambda: send(0, k, h, z, SIB))
+            pl.when((z == 0) | (z == last))(lambda: send(0, k, h, z, FAR))
 
     def take_r(k, h):
         lo = low(k)
@@ -140,6 +173,8 @@
                     def arrive(s=s, d=d):
                         received(0, k, h, s, c)
                         onward = (z + 1 <= hi) if d == 1 else (z - 1 >= lo)
+                        if lo == 1:
+                            onward &= ((s > 0) | (z > 1)) if d == 1 else ((s < last) | (z < last - 1))
                         pl.when(onward)(lambda: send(0, k, h, s, UP if d == 1 else DOWN))
                         send(0, k, h, s, SIB)
 
@@ -172,7 +207,8 @@
         def for_end():
             n = k - FULL_STEPS
             if h == 0:
-                end_copy(k, z).wait_recv()
+                for t in range(1, sharers):
+                    share(k, t).wait_recv()
             end = jnp.where(z == lo, 0, last)
             gathered = rbuf[k, h].reshape(ranks * rows, cols)
             xbuf[k, h, 2 * end + c] = mm(end_inv[n], gathered).astype(BF16)
@@ -261,19 +297,26 @@
         pl.when(z == 0)(lambda k=k: end_copy(k, 1).start())
         pl.when(z == last)(lambda k=k: end_copy(k, last - 1).start())
 
-    pending = None
+    pending = []
     for k in range(steps):
         for h in range(halves):
             take_r(k, h)
             solve(k, h)
-            if pending is not None:
-                finish(*pending)
-                sensitivity(*pending)
+        if k == 0:
+            share_end(FULL_STEPS)
+        for h in range(halves):
+            if pending:
+                finish(*pending[h])
+                sensitivity(*pending[h])
             take_x(k, h)
             if k + 1 < steps:
                 next_r(k, h)
-            pending = (k, h)
-    sensitivity(*pending)
+        if k == 0:
+            for n in range(FULL_STEPS + 1, steps):
+                share_end(n)
+        pending = [(k, h) for h in range(halves)]
+    for phase in pending:
+        sensitivity(*phase)
     sens[mine] = sacc[...]
     shares = []
     for t in range(1, peers):
@@ -285,7 +328,8 @@
         )
         copy.start()
         shares.append(copy)
-    finish(*pending)
+    for phase in pending:
+        finish(*phase)
     for copy in shares:
         copy.wait()
     total = sens[0]
@@ -307,8 +351,11 @@
             return lambda: shard(kind, k, h, index, direction).wait_send()
 
         pl.when((z >= lo) & (z <= hi))(left(0, SIB))
-        pl.when((s <= z) & (z + 1 <= hi))(left(0, UP))
-        pl.when((s >= z) & (z - 1 >= lo))(left(0, DOWN))
+        skip_up = (lo == 1) & (s == 0) & (z == 1)
+        skip_down = (lo == 1) & (s == last) & (z == last - 1)
+        pl.when((s <= z) & (z + 1 <= hi) & jnp.logical_not(skip_up))(left(0, UP))
+        pl.when((s >= z) & (z - 1 >= lo) & jnp.logical_not(skip_down))(left(0, DOWN))
+        pl.when((lo == 1) & (s == z) & ((z == 0) | (z == last)))(left(0, FAR))
         left(1, SIB)()
         pl.when((home <= z) & (z + 1 <= last))(left(1, UP))
         pl.when((home >= z) & (z - 1 >= 0))(left(1, DOWN))
@@ -317,6 +364,12 @@
     lax.fori_loop(0, steps * halves * chips, drain, 0)
     for k in range(FULL_STEPS, steps):
         pl.when((z == 0) | (z == last))(lambda k=k: end_copy(k, 1).wait_send())
+
+        def left_share(k=k):
+            for t in range(1, sharers):
+                share(k, t).wait_send()
+
+        pl.when((z == 1) | (z == last - 1))(left_share)
     for copy in stores:
         copy.wait()
 
@@ -359,7 +412,8 @@
             dma((2, ends)),
             dma((steps, HALVES, ranks)),
             dma((steps, HALVES, ranks)),
-            dma((2, steps, HALVES, ranks, 3)),
+            dma((2, steps, HALVES, ranks, 4)),
+            dma((2, ends, peers)),
             dma((peers,)),
             dma((peers,)),
         ],

time: 192 us -> 139 us (0.72)
  Pallas kernels: 182 us -> 129 us
    pallas_call x1, Pallas kernels: 182 us -> 129 us  [local(): pl.pallas_call(functools.partial(kernel, chips, peers), out_shape=(jax.Sh...]
where the time goes in v2:
time: 139 us
  Pallas kernels  129 us (93%)
  local copies, waits for them, and re-layouts  9.27 us (7%)
    pallas_call x1, Pallas kernels, local(): pl.pallas_call(functools.partial(kernel, chips, peers), out_shape=(jax.Sh...  129 us
    unnamed x3, local copies, waits for them, and re-layouts  8.37 us

profile of v2, /device:TPU:0, one launch (start us, length us, event | category | flops | bytes accessed | tf_op | source)
XLA Modules:
  0.0 138.7 jit_solution(14161954796769557645)
XLA Ops:
  0.6 128.8 %substitution.1 = (f32[4,192,512]{2,1,0:T(8,128)}, f32[12,192,512]{2,1,0:T(8,128)}, f32[192,128]{1,0:T(8,128)}) custom-call(bf16[16,192,6144]{2,1,0:T(8,128)(2,1)} %factor.1, bf16[4,192,1536]{2,1,0:T(8,128)(2,1)} %inverse.1, f32[16,192,512]{2,1,0:T(8,128)} %right.1, f32[4,192,512]{2,1,0:T(8,128)} %deriv.1), custom_call_target="tpu_custom_call" | custom-call | flops 17515413504 | bytes 52690944 | tf_op jit(solution)/shard_map/substitution/pallas_call | solution.py:388
  129.4 0.9 slice_bitcast_fusion
  130.3 0.7 copy.7
  131.0 2.7 %copy.10 = f32[4,192,512]{2,1,0:T(8,128)} copy(f32[4,192,512]{2,1,0:T(8,128)} %get-tuple-element.15) | data formatting | bytes 3145728
  133.7 5.0 %copy.11 = f32[12,192,512]{2,1,0:T(8,128)} copy(f32[12,192,512]{2,1,0:T(8,128)} %get-tuple-element.16) | data formatting | bytes 9437184

commit v3 on v2

--- a/solution.py
+++ b/solution.py
@@ -21,7 +21,7 @@
 def kernel(
     chips, peers,
     factor, inverse, right, deriv,
-    solved_out, trailing_out, sens_out,
+    solved_out, part_out, last_out, sens_out,
     panel, inv, end_inv, tail, racc, tacc, sd, sol, rbuf, xbuf, sacc, sens,
     load_sem, store_sem, end_sem, r_recv, x_recv, send_sem, share_sem, peer_send, peer_recv,
 ):
@@ -278,15 +278,40 @@
             return carry
 
         lax.fori_loop(0, blocks // group, update, 0)
-        if k == steps - 1:
-            store(tacc.at[h], trailing_out.at[:, :, columns(h)])
+        if k == steps - (2 if h == halves - 1 else 1):
+            store(tacc.at[h], part_out.at[:, :, columns(h)])
 
     def sensitivity(k, h):
         ready(("d", h))
         store(sol.at[h, k], solved_out.at[k, :, columns(h)])
         part = jnp.sum(sol[h, k] * sd[h, k], axis=1, keepdims=True)
         lane = lax.broadcasted_iota(jnp.int32, (rows, 128), 1)
-        sacc[...] += jnp.where(lane == k, part, 0.0)
+        sacc[pl.ds(0, rows)] += jnp.where(lane == k, part, 0.0)
+
+    def drain(k, n, carry):
+        h = n // chips
+        s = lax.rem(n, chips)
+        lo = jnp.int32(low(k))
+        hi = last - lo
+        home = jnp.clip(s, lo, hi)
+        index = 2 * s + c
+
+        def left(kind, direction):
+            return lambda: shard(kind, k, h, index, direction).wait_send()
+
+        pl.when((z >= lo) & (z <= hi))(left(0, SIB))
+        skip_up = (lo == 1) & (s == 0) & (z == 1)
+        skip_down = (lo == 1) & (s == last) & (z == last - 1)
+        pl.when((s <= z) & (z + 1 <= hi) & jnp.logical_not(skip_up))(left(0, UP))
+        pl.when((s >= z) & (z - 1 >= lo) & jnp.logical_not(skip_down))(left(0, DOWN))
+        pl.when((lo == 1) & (s == z) & ((z == 0) | (z == last)))(left(0, FAR))
+        left(1, SIB)()
+        pl.when((home <= z) & (z + 1 <= last))(left(1, UP))
+        pl.when((home >= z) & (z - 1 >= 0))(left(1, DOWN))
+        return carry
+
+    def drain_step(k):
+        lax.fori_loop(0, halves * chips, functools.partial(drain, k), 0)
 
     sacc[...] = jnp.zeros_like(sacc)
     for h in range(halves):
@@ -304,20 +329,28 @@
             solve(k, h)
         if k == 0:
             share_end(FULL_STEPS)
+        else:
+            drain_step(k - 1)
         for h in range(halves):
-            if pending:
-                finish(*pending[h])
-                sensitivity(*pending[h])
+            if k == steps - 1 and h > 0:
+                finish(k, h - 1)
+            for phase in pending[h:] if k < steps - 1 or h == 0 else []:
+                finish(*phase)
+                sensitivity(*phase)
+                if k < steps - 1:
+                    break
             take_x(k, h)
             if k + 1 < steps:
                 next_r(k, h)
+            else:
+                if h == halves - 1:
+                    store(xbuf.at[k, h], last_out)
+                sensitivity(k, h)
         if k == 0:
             for n in range(FULL_STEPS + 1, steps):
                 share_end(n)
         pending = [(k, h) for h in range(halves)]
-    for phase in pending:
-        sensitivity(*phase)
-    sens[mine] = sacc[...]
+    sens[mine] = sacc[...].T[: sens.shape[1]]
     shares = []
     for t in range(1, peers):
         copy = pltpu.make_async_remote_copy(
@@ -328,8 +361,7 @@
         )
         copy.start()
         shares.append(copy)
-    for phase in pending:
-        finish(*phase)
+    drain_step(steps - 1)
     for copy in shares:
         copy.wait()
     total = sens[0]
@@ -337,31 +369,6 @@
         total = total + sens[j]
     sens_out[...] = total
 
-    def drain(n, carry):
-        p = n // chips
-        s = lax.rem(n, chips)
-        k = p // halves
-        h = lax.rem(p, halves)
-        lo = jnp.where(k < FULL_STEPS, 0, 1)
-        hi = last - lo
-        home = jnp.clip(s, lo, hi)
-        index = 2 * s + c
-
-        def left(kind, direction):
-            return lambda: shard(kind, k, h, index, direction).wait_send()
-
-        pl.when((z >= lo) & (z <= hi))(left(0, SIB))
-        skip_up = (lo == 1) & (s == 0) & (z == 1)
-        skip_down = (lo == 1) & (s == last) & (z == last - 1)
-        pl.when((s <= z) & (z + 1 <= hi) & jnp.logical_not(skip_up))(left(0, UP))
-        pl.when((s >= z) & (z - 1 >= lo) & jnp.logical_not(skip_down))(left(0, DOWN))
-        pl.when((lo == 1) & (s == z) & ((z == 0) | (z == last)))(left(0, FAR))
-        left(1, SIB)()
-        pl.when((home <= z) & (z + 1 <= last))(left(1, UP))
-        pl.when((home >= z) & (z - 1 >= 0))(left(1, DOWN))
-        return carry
-
-    lax.fori_loop(0, steps * halves * chips, drain, 0)
     for k in range(FULL_STEPS, steps):
         pl.when((z == 0) | (z == last))(lambda k=k: end_copy(k, 1).wait_send())
 
@@ -372,6 +379,47 @@
         pl.when((z == 1) | (z == last - 1))(left_share)
     for copy in stores:
         copy.wait()
+
+
+def last_kernel(tail, spread, part, solved, trailing_out, solved_out):
+    blocks, rows, size = tail.shape
+    product = mm(tail[...].reshape(blocks * rows, size), spread[...].reshape(size, spread.shape[2]))
+    done = part.shape[2] - spread.shape[2]
+    trailing_out[:, :, :done] = part[:, :, :done]
+    trailing_out[:, :, done:] = part[:, :, done:] - product.reshape(blocks, rows, spread.shape[2])
+    solved_out[...] = solved[...]
+
+
+def add_last(factor, spread, part, solved):
+    steps, rows, width = solved.shape
+    blocks = part.shape[0]
+    size = spread.shape[0] * rows
+    group = 2 if steps % 2 == 0 and blocks % 2 == 0 else 1
+    final = steps // group - 1
+    one = lambda i: (i, 0, 0)
+    kept = lambda i: (jnp.minimum(i, final), 0, 0)
+    wide = (group, rows, width)
+    return pl.pallas_call(
+        last_kernel,
+        grid=(blocks // group,),
+        in_specs=[
+            pl.BlockSpec((group, rows, size), lambda i: (steps // group + i, 0, steps - 1)),
+            pl.BlockSpec(spread.shape, lambda i: (0, 0, 0)),
+            pl.BlockSpec(wide, one),
+            pl.BlockSpec(wide, kept),
+        ],
+        out_specs=(pl.BlockSpec(wide, one), pl.BlockSpec(wide, kept)),
+        out_shape=(
+            jax.ShapeDtypeStruct(part.shape, F32), jax.ShapeDtypeStruct(solved.shape, F32)
+        ),
+        compiler_params=pltpu.CompilerParams(vmem_limit_bytes=63 * 1024 * 1024),
+        cost_estimate=pl.CostEstimate(
+            flops=2 * blocks * rows * size * spread.shape[2],
+            bytes_accessed=2 * blocks * rows * size + 8 * part.size + 8 * solved.size,
+            transcendentals=0,
+        ),
+        name="last_block",
+    )(factor, spread, part, solved)[::-1]
 
 
 def local(chips, peers, factor, inverse_blocks, right_side, shape_derivative):
@@ -382,18 +430,22 @@
     ranks = 2 * chips
     pairs = steps * (steps - 1) // 2
     ends = steps - FULL_STEPS
-    multiplied = (pairs + steps * blocks) * rows * size * width + steps * rows * size * width
+    padded = -(-rows // 128) * 128
+    lines = -(-steps // 8) * 8
+    early = steps - 1
+    multiplied = (pairs + early * blocks + steps) * rows * size * width
     anywhere = pl.BlockSpec(memory_space=pl.ANY)
     dma = pltpu.SemaphoreType.DMA
-    solved, trailing, sens = pl.pallas_call(
+    solved, part, spread, sens = pl.pallas_call(
         functools.partial(kernel, chips, peers),
         out_shape=(
             jax.ShapeDtypeStruct((steps, rows, width), F32),
             jax.ShapeDtypeStruct((blocks, rows, width), F32),
-            jax.ShapeDtypeStruct((rows, 128), F32),
+            jax.ShapeDtypeStruct((ranks, rows, cols), BF16),
+            jax.ShapeDtypeStruct((lines, padded), F32),
         ),
         in_specs=[anywhere] * 4,
-        out_specs=(anywhere, anywhere, pl.BlockSpec(memory_space=pltpu.VMEM)),
+        out_specs=(anywhere, anywhere, anywhere, pl.BlockSpec(memory_space=pltpu.VMEM)),
         scratch_shapes=[
             pltpu.VMEM((pairs, rows, size), BF16),
             pltpu.VMEM((steps, rows, size), BF16),
@@ -405,10 +457,10 @@
             pltpu.VMEM((HALVES, steps, rows, cols), F32),
             pltpu.VMEM((steps, HALVES, ranks, rows, cols), BF16),
             pltpu.VMEM((steps, HALVES, ranks, rows, cols), BF16),
-            pltpu.VMEM((rows, 128), F32),
-            pltpu.VMEM((peers, rows, 128), F32),
+            pltpu.VMEM((padded, 128), F32),
+            pltpu.VMEM((peers, lines, padded), F32),
             dma((pairs + 2 * steps + 3 * HALVES,)),
-            dma((steps * HALVES + HALVES,)),
+            dma((steps * HALVES + HALVES + 1,)),
             dma((2, ends)),
             dma((steps, HALVES, ranks)),
             dma((steps, HALVES, ranks)),
@@ -427,7 +479,8 @@
         ),
         name="substitution",
     )(factor, inverse_blocks, right_side, shape_derivative)
-    return solved, trailing, sens[:, :steps].T
+    solved, trailing = add_last(factor, spread, part, solved)
+    return solved, trailing, sens[:steps, :rows]
 
 
 def solution(mesh):

time: 139 us -> 137 us (0.986)
  local copies, waits for them, and re-layouts: 9.27 us -> 0.6 us
  Pallas kernels: 129 us -> 136 us
    pallas_call x0 -> x1, Pallas kernels: none -> 9.99 us  [add_last(): pl.pallas_call(last_kernel, grid=(blocks // group,), in_specs=[pl.BlockSp...]
    unnamed x3 -> x2, local copies, waits for them, and re-layouts: 8.37 us -> 0.01 us
    pallas_call x1, Pallas kernels: 129 us -> 126 us  [local(): pl.pallas_call(functools.partial(kernel, chips, peers), out_shape=(jax.Sh...]
where the time goes in v3:
time: 137 us
  Pallas kernels  136 us (99%)
    pallas_call x1, Pallas kernels, local(): pl.pallas_call(functools.partial(kernel, chips, peers), out_shape=(jax.Sh...  126 us
    pallas_call x1, Pallas kernels, add_last(): pl.pallas_call(last_kernel, grid=(blocks // group,), in_specs=[pl.BlockSp...  9.99 us

profile of v3, /device:TPU:0, one launch (start us, length us, event | category | flops | bytes accessed | tf_op | source)
XLA Modules:
  0.0 136.8 jit_solution(11320771164566890000)
XLA Ops:
  0.6 125.5 %substitution.1 = (f32[4,192,512]{2,1,0:T(8,128)}, f32[12,192,512]{2,1,0:T(8,128)}, bf16[8,192,256]{2,1,0:T(8,128)(2,1)}, f32[8,256]{1,0:T(8,128)}) custom-call(bf16[16,192,6144]{2,1,0:T(8,128)(2,1)} %tail.1, bf16[4,192,1536]{2,1,0:T(8,128)(2,1)} %inverse.1, f32[16,192,512]{2,1,0:T(8,128)} %right.1, f32[4,192,512]{2,1,0:T(8,128)} %deriv.1), custom_call_target="tpu_custom_call" | custom-call | flops 13891534848 | bytes 52690944 | tf_op jit(solution)/shard_map/substitution/pallas_call | solution.py:439
  126.2 0.0 copy-start
  126.2 10.0 %last_block.1 = (f32[12,192,512]{2,1,0:T(8,128)}, f32[4,192,512]{2,1,0:T(8,128)}) custom-call(bf16[16,192,6144]{2,1,0:T(8,128)(2,1)} %tail.1, bf16[8,192,256]{2,1,0:T(8,128)(2,1)} %get-tuple-element.9.spread, f32[12,192,512]{2,1,0:T(8,128)} %get-tuple-element.10.part, f32[4,192,512]{2,1,0:T(8,128)} %get-tuple-element.11.solved), custom_call_target="tpu_custom_call" | custom-call | flops 1811939328 | bytes 19660800 | tf_op jit(solution)/shard_map/last_block/pallas_call | solution.py:402
  136.2 0.0 copy-done
  136.2 0.6 slice.3
Async XLA Ops:
  126.2 10.0 %copy-start = (f32[8,256]{1,0:T(8,128)S(1)}, f32[8,256]{1,0:T(8,128)}, u32[]{:S(2)}) copy-start(f32[8,256]{1,0:T(8,128)} %get-tuple-element.14) | copy-start | bytes 24580
